TPU v7x, 256 devices: a whole 4x4x8 slice. The times are simulated.
256 devices in a mesh: out: 16 (over y, x), inp: 16 (over z, core).
Axes of the slice: x: 4, y: 4, z: 8, core: 2. Of those that a mesh axis runs over, the one named last changes fastest.
Arguments:
- grads: bfloat16 [2048, 28672], P('out', 'inp'), may hold values from -1.1953125 to 1.1953125
- acts: bfloat16 [2048, 8192], P('inp', 'out'), may hold values from -6 to 6
- basis_out: bfloat16 [28672, 14336], P('inp', 'out'), may hold values from -0.03125 to 0.03125
- basis_in: bfloat16 [8192, 8192], P('out', 'inp'), may hold values from -0.0625 to 0.0625
- old_correction: float32 [14336, 8192], P('out', 'inp'), may hold values from 0.1 to 2
- lengths: int32 [16], replicated, may hold values from 1 to 256, 2048 in all
Outputs:
- correction: float32 [14336, 8192], P('out', 'inp')
Inputs may be any that keep to these rules, and one draw needn't show every extreme that they name: The lengths sum to 2048; the longest example has exactly 256 tokens.
All inputs are finite; a program needn't handle non-finite values.
Results may differ from a plain program's by a relative error of at most 0.0021.
Values may be sent and summed in bfloat16 or wider, within the bound.
No kernel may reach another device: no remote copies, remote signals or barrier semaphores. Data moves between devices by JAX's collectives and lax.ppermute only.
A program may use at most 128 MiB of HBM per device.

v0:
```python
import jax
import jax.numpy as jnp
from jax import lax
from jax.sharding import PartitionSpec as P

CAP = 256


def body(grads, acts, basis_out, basis_in, old_correction, lengths):
    gathered = lax.all_gather(grads, "out", axis=0, tiled=True)
    row_count = gathered.shape[0]
    scattered = lax.psum_scatter(
        lax.dot_general(
            basis_out, gathered, (((0,), (1,)), ((), ())), preferred_element_type=jnp.float32
        ),
        "inp",
        scatter_dimension=0,
        tiled=True,
    )
    grad_rot = lax.all_gather(scattered.astype(jnp.bfloat16), "inp", axis=0, tiled=True)
    token_dim = 1
    gathered_acts = lax.all_gather(acts, "inp", axis=0, tiled=True)
    act_scattered = lax.psum_scatter(
        jnp.dot(gathered_acts, basis_in, preferred_element_type=jnp.float32),
        "out",
        scatter_dimension=0,
        tiled=True,
    )
    act_rot = lax.all_gather(act_scattered.astype(jnp.bfloat16), "out", axis=0, tiled=True)
    offsets = jnp.cumsum(lengths) - lengths
    examples = lengths.shape[0]

    def add_example(example, running):
        offset = offsets[example]
        length = lengths[example]
        first_row = jnp.minimum(offset, row_count - CAP)
        places = first_row + jnp.arange(CAP, dtype=jnp.int32)
        inside = (places >= offset) & (places < offset + length)
        grad_block = lax.dynamic_slice_in_dim(grad_rot, first_row, CAP, token_dim)
        act_block = lax.dynamic_slice_in_dim(act_rot, first_row, CAP, 0)
        act_block = jnp.where(inside[:, None], act_block, jnp.zeros((), act_block.dtype))
        projected = lax.dot_general(
            grad_block,
            act_block,
            (((token_dim,), (0,)), ((), ())),
            preferred_element_type=jnp.float32,
        )
        return running + projected * projected

    running = lax.fori_loop(0, examples, add_example, jnp.zeros(old_correction.shape, jnp.float32))
    return 0.8 * old_correction + 0.2 * running / examples


def solution(mesh):
    in_specs = (
        P("out", "inp"),
        P("inp", "out"),
        P("inp", "out"),
        P("out", "inp"),
        P("out", "inp"),
        P(),
    )
    out_specs = P("out", "inp")
    return jax.shard_map(body, mesh=mesh, in_specs=in_specs, out_specs=out_specs, check_vma=False)
```

profile of v0, /device:TPU:1, one launch (start us, length us, event | category | flops | bytes accessed | tf_op | source)
XLA Modules:
  0.0 505.1 jit_solution(16237639878966446037)
XLA Ops:
  6.5 0.7 all-gather.9.cloned.1.call-update
  7.3 0.7 all-gather.5.cloned.1.call-update
  8.1 45.1 %all-gather.9.cloned.1.call-done = bf16[2048,512]{1,0:T(8,128)(2,1)} async-done(((bf16[128,512]{1,0:T(8,128)(2,1)}), bf16[2048,512]{1,0:T(8,128)(2,1)}) %all-gather.9.cloned.1.call-update) | async-done | bytes 2097168 | tf_op jit(solution)/shard_map/all_gather | solution.py:22
  53.2 4.9 fusion.8
  58.1 66.5 %all-gather.5.cloned.1.call-done = bf16[2048,1792]{1,0:T(8,128)(2,1)} async-done(((bf16[128,1792]{1,0:T(8,128)(2,1)}), bf16[2048,1792]{1,0:T(8,128)(2,1)}) %all-gather.5.cloned.1.call-update) | async-done | bytes 7340048 | tf_op jit(solution)/shard_map/all_gather | solution.py:10
  124.7 10.9 %fusion.7 = f32[896,2048]{1,0:T(8,128)} fusion(bf16[1792,896]{1,0:T(8,128)(2,1)S(1)} %copy-done, bf16[2048,1792]{1,0:T(8,128)(2,1)} %all-gather.5.cloned.1.call-done), kind=kOutput, calls=%fused_computation.10 | convolution fusion | flops 6576668672 | bytes 17891328 | tf_op jit(solution)/shard_map/dot_general | solution.py:13
  135.7 73.4 %reduce-scatter.5.cloned.1.call-done = f32[128,512]{1,0:T(8,128)} async-done(((f32[2048,512]{1,0:T(8,128)}), f32[128,512]{1,0:T(8,128)}) %reduce-scatter.5.cloned.1.call-update) | async-done | bytes 262160 | tf_op jit(solution)/shard_map/reduce_scatter | solution.py:23
  209.1 1.6 convert_element_type.7
  210.8 67.7 %reduce-scatter.3.cloned.1.call-done = f32[56,2048]{1,0:T(8,128)} async-done(((f32[896,2048]{1,0:T(8,128)}), f32[56,2048]{1,0:T(8,128)}) %reduce-scatter.3.cloned.1.call-update) | async-done | bytes 458768 | tf_op jit(solution)/shard_map/reduce_scatter | solution.py:12
  278.4 1.7 convert_element_type.6
  280.5 51.2 %all-gather.11.cloned.1.call-done = bf16[2048,512]{1,0:T(8,128)(2,1)} async-done(((bf16[128,512]{1,0:T(8,128)(2,1)}), bf16[2048,512]{1,0:T(8,128)(2,1)}) %all-gather.11.cloned.1.call-update) | async-done | bytes 2097168 | tf_op jit(solution)/shard_map/all_gather | solution.py:29
  331.6 44.1 %all-gather.7.cloned.1.call-done = bf16[896,2048]{1,0:T(8,128)(2,1)} async-done(((bf16[56,2048]{1,0:T(8,128)(2,1)}), bf16[896,2048]{1,0:T(8,128)(2,1)}) %all-gather.7.cloned.1.call-update) | async-done | bytes 3670032 | tf_op jit(solution)/shard_map/all_gather | solution.py:20
  375.7 118.8 %while.14 = (s32[]{:T(128)}, f32[896,512]{1,0:T(8,128)}, s32[16]{0:T(128)S(1)}, bf16[896,2048]{1,0:T(8,128)(2,1)}, s32[16]{0:T(128)S(1)}, /*index=5*/bf16[2048,5...) while((s32[]{:T(128)}, f32[896,512]{1,0:T(8,128)}, s32[16]{0:T(128)S(1)}, ...), condition=%wide.region_4.5_spmd.clone, body=%wide.region_3.4_spmd.clone.sunk | while | flops 236389376 | bytes 4393164 | solution.py:50
  379.0 0.7 compare_and_fusion.2
  379.7 2.9 select_add_fusion.2
  385.8 0.7 compare_and_fusion.2
  386.5 3.5 select_add_fusion.2
  393.3 0.7 compare_and_fusion.2
  394.0 3.5 select_add_fusion.2
  400.8 0.7 compare_and_fusion.2
  401.5 3.5 select_add_fusion.2
  405.0 0.7 dynamic_slice.44
  408.2 0.7 compare_and_fusion.2
  408.9 3.5 select_add_fusion.2
  415.7 0.7 compare_and_fusion.2
  416.4 3.5 select_add_fusion.2
  423.2 0.7 compare_and_fusion.2
  423.9 3.5 select_add_fusion.2
  430.7 0.7 compare_and_fusion.2
  431.4 3.5 select_add_fusion.2
  438.2 0.7 compare_and_fusion.2
  438.9 3.5 select_add_fusion.2
  445.6 0.7 compare_and_fusion.2
  446.3 3.5 select_add_fusion.2
  453.1 0.7 compare_and_fusion.2
  453.8 3.5 select_add_fusion.2
  460.6 0.7 compare_and_fusion.2
  461.3 3.5 select_add_fusion.2
  468.1 0.7 compare_and_fusion.2
  468.8 3.5 select_add_fusion.2
  475.5 0.7 compare_and_fusion.2
  476.3 3.5 select_add_fusion.2
  479.7 0.7 dynamic_slice.44
  483.0 0.7 compare_and_fusion.2
  483.7 3.5 select_add_fusion.2
  490.4 0.7 compare_and_fusion.2
  491.1 3.5 select_add_fusion.2
  494.6 3.7 multiply_add_fusion
  (49 shorter events, 19.3 us)
Async XLA Ops:
  6.5 118.1 %copy-start = (bf16[1792,896]{1,0:T(8,128)(2,1)S(1)}, bf16[1792,896]{1,0:T(8,128)(2,1)}, u32[]{:S(2)}) copy-start(bf16[1792,896]{1,0:T(8,128)(2,1)} %param.10) | copy-start | bytes 9633796
  6.5 46.6 %all-gather.9.cloned.1.call-start = ((), (), s32[]{:S(2)}) async-start(), calls=%async_computation.5 | async-start | bytes 2228224 | tf_op jit(solution)/shard_map/all_gather | solution.py:22
  7.3 117.4 %all-gather.5.cloned.1.call-start = ((), (), s32[]{:S(2)}) async-start(), calls=%async_computation.2 | async-start | bytes 7798784 | tf_op jit(solution)/shard_map/all_gather | solution.py:10
  8.0 201.1 %reduce-scatter.5.cloned.1.call-start = ((), (), s32[]{:S(2)}) async-start(), calls=%async_computation.6 | async-start | bytes 4456448 | tf_op jit(solution)/shard_map/reduce_scatter | solution.py:23
  58.1 220.3 %reduce-scatter.3.cloned.1.call-start = ((), (), s32[]{:S(2)}) async-start(), calls=%async_computation.3 | async-start | bytes 7798784 | tf_op jit(solution)/shard_map/reduce_scatter | solution.py:12
  135.6 144.6 %copy-start.1 = (s32[16]{0:T(128)S(1)}, s32[16]{0:T(128)}, u32[]{:S(2)}) copy-start(s32[16]{0:T(128)} %param.13) | copy-start | bytes 196
  135.6 196.0 %all-gather.11.cloned.1.call-start = ((), (), s32[]{:S(2)}) async-start(), calls=%async_computation.7 | async-start | bytes 2228224 | tf_op jit(solution)/shard_map/all_gather | solution.py:29
  210.7 165.0 %all-gather.7.cloned.1.call-start = ((), (), s32[]{:S(2)}) async-start(), calls=%async_computation.4 | async-start | bytes 3899392 | tf_op jit(solution)/shard_map/all_gather | solution.py:20
Sparse Core Ops, SparseCore 0:
  9.2 43.9 all-gather.8
  55.6 69.0 all-gather.4
  128.3 80.7 reduce-scatter.4
  211.7 66.7 reduce-scatter.2
  281.0 50.5 all-gather.10
  333.5 42.2 all-gather.6
where the time goes:
time: 506 us; the launch traced here: 505 us
  waiting for transfers between devices  349 us (69%)
  matrix products  71.7 us (14%)
  loops' own time  31.7 us (6%)
  local copies, waits for them, and re-layouts  20.2 us (4%)
  other arithmetic  18.3 us (4%)
  between operations  13.5 us (3%)
    reduce_scatter x1, waiting for transfers between devices, body(): lax.psum_scatter(jnp.dot(gathered_acts, basis_in, preferred_element_type=...  73.4 us
    reduce_scatter x1, waiting for transfers between devices, body(): lax.psum_scatter(lax.dot_general(basis_out, gathered, (((0,), (1,)), ((),...  67.7 us
    all_gather x1, waiting for transfers between devices, body(): gathered = lax.all_gather(grads, 'out', axis=0, tiled=True)  66.5 us
    dot_general x16, matrix products, add_example(): lax.dot_general(grad_block, act_block, (((token_dim,), (0,)), ((), ())),...  55.9 us
    all_gather x1, waiting for transfers between devices, body(): lax.all_gather(act_scattered.astype(jnp.bfloat16), 'out', axis=0, tiled=T...  51.2 us
    all_gather x1, waiting for transfers between devices, body(): gathered_acts = lax.all_gather(acts, 'inp', axis=0, tiled=True)  45.1 us
    all_gather x1, waiting for transfers between devices, body(): lax.all_gather(scattered.astype(jnp.bfloat16), 'inp', axis=0, tiled=True)  44.1 us
    another operation x1, loops' own time, body(): lax.fori_loop(0, examples, add_example, jnp.zeros(old_correction.shape, j...  31.7 us
  transfers between devices with their start and end apart: 6, of which 6 were waited for; matrix products, arithmetic and copies ran while one was open for 4% of the time, Pallas kernels for 0%

commit v1 on v0

--- a/solution.py
+++ b/solution.py
@@ -6,8 +6,26 @@
 CAP = 256
 
 
+def joined_along(tiles, dim):
+    tiles = jnp.moveaxis(tiles, 0, dim)
+    shape = tiles.shape
+    return tiles.reshape(*shape[:dim], shape[dim] * shape[dim + 1], *shape[dim + 2 :])
+
+
 def body(grads, acts, basis_out, basis_in, old_correction, lengths):
-    gathered = lax.all_gather(grads, "out", axis=0, tiled=True)
+    peers = lax.axis_size("out")
+    pairs = [(i, (i + 1) % peers) for i in range(peers)]
+    back = [(b, a) for a, b in pairs]
+    lower, upper = ([], [])
+    for step in range(peers - 1):
+        if step % 2 == 0:
+            lower.append(lax.ppermute(lower[-1] if lower else grads, "out", pairs))
+        else:
+            upper.append(lax.ppermute(upper[-1] if upper else grads, "out", back))
+    parts = jnp.stack([*lower[::-1], grads, *upper])
+    shift = lax.axis_index("out") - len(lower)
+    parts = parts[(jnp.arange(peers) - shift) % peers]
+    gathered = joined_along(parts, 0)
     row_count = gathered.shape[0]
     scattered = lax.psum_scatter(
         lax.dot_general(

time: 506 us -> 498 us (0.984)
  waiting for transfers between devices: 349 us -> 259 us
  local copies, waits for them, and re-layouts: 20.2 us -> 65.1 us
  starting transfers between devices: 0.2 us -> 37.6 us
    all_gather x1 -> x0, waiting for transfers between devices: 66.5 us -> none  [body(): gathered = lax.all_gather(grads, 'out', axis=0, tiled=True)]
    ppermute x0 -> x15, waiting for transfers between devices: none -> 57.6 us  [the longest x8 53.8 us: body(): lower.append(lax.ppermute(lower[-1] if lower else grads, 'out', pairs))]
    all_gather x1, waiting for transfers between devices: 45.1 us -> 0.01 us  [body(): gathered_acts = lax.all_gather(acts, 'inp', axis=0, tiled=True)]
    ppermute x0 -> x15, starting transfers between devices: none -> 37.4 us  [the longest x7 35.4 us: body(): upper.append(lax.ppermute(upper[-1] if upper else grads, 'out', back))]
    unnamed x4 -> x42, local copies, waits for them, and re-layouts: 0.01 us -> 35.6 us
    reduce_scatter x1, waiting for transfers between devices: 73.4 us -> 38.6 us  [body(): lax.psum_scatter(jnp.dot(gathered_acts, basis_in, preferred_element_type=...]
    gather x0 -> x1, local copies, waits for them, and re-layouts: none -> 7.15 us  [body(): parts = parts[(jnp.arange(peers) - shift) % peers]]
  transfers between devices with their start and end apart: 6 -> 20, of which waited for: 6 -> 16; matrix products, arithmetic and copies ran while one was open for 4% -> 13% of each run, Pallas kernels for 0% -> 0%
where the time goes in v1:
time: 498 us; the launch traced here: 496 us
  waiting for transfers between devices  259 us (52%)
  matrix products  72.8 us (15%)
  local copies, waits for them, and re-layouts  65.1 us (13%)
  starting transfers between devices  37.6 us (8%)
  loops' own time  30.9 us (6%)
  other arithmetic  17 us (3%)
  between operations  13.2 us (3%)
    reduce_scatter x1, waiting for transfers between devices, body(): lax.psum_scatter(lax.dot_general(basis_out, gathered, (((0,), (1,)), ((),...  67.8 us
    dot_general x16, matrix products, add_example(): lax.dot_general(grad_block, act_block, (((token_dim,), (0,)), ((), ())),...  55.9 us
    ppermute x8, waiting for transfers between devices, body(): lower.append(lax.ppermute(lower[-1] if lower else grads, 'out', pairs))  53.8 us
    all_gather x1, waiting for transfers between devices, body(): lax.all_gather(act_scattered.astype(jnp.bfloat16), 'out', axis=0, tiled=T...  51.2 us
    all_gather x1, waiting for transfers between devices, body(): lax.all_gather(scattered.astype(jnp.bfloat16), 'inp', axis=0, tiled=True)  44.1 us
    reduce_scatter x1, waiting for transfers between devices, body(): lax.psum_scatter(jnp.dot(gathered_acts, basis_in, preferred_element_type=...  38.6 us
    unnamed x42, local copies, waits for them, and re-layouts  35.6 us
    ppermute x7, starting transfers between devices, body(): upper.append(lax.ppermute(upper[-1] if upper else grads, 'out', back))  35.4 us
  transfers between devices with their start and end apart: 20, of which 16 were waited for; matrix products, arithmetic and copies ran while one was open for 13% of the time, Pallas kernels for 0%

profile of v1, /device:TPU:1, one launch (start us, length us, event | category | flops | bytes accessed | tf_op | source)
XLA Modules:
  0.0 496.1 jit_solution(2947978650718330207)
XLA Ops:
  6.5 2.0 collective-permute-start
  8.6 12.3 %collective-permute-done = bf16[128,1792]{1,0:T(8,128)(2,1)} collective-permute-done((bf16[128,1792]{1,0:T(8,128)(2,1)}, bf16[128,1792]{1,0:T(8,128)(2,1)}, u32[]{:S(2)}, u32[]{:S(2)}) %collective-permute-start) | collective-permute-done | bytes 458784 | tf_op jit(solution)/shard_map/ppermute | solution.py:22
  21.0 4.9 collective-permute-start.8
  25.8 7.5 %collective-permute-done.1 = bf16[128,1792]{1,0:T(8,128)(2,1)} collective-permute-done((bf16[128,1792]{1,0:T(8,128)(2,1)}, bf16[128,1792]{1,0:T(8,128)(2,1)}, u32[]{:S(2)}, u32[]{:S(2)}) %collective-permute-start.1) | collective-permute-done | bytes 458784 | tf_op jit(solution)/shard_map/ppermute | solution.py:22
  34.2 4.8 collective-permute-start.9
  38.9 5.9 %collective-permute-done.2 = bf16[128,1792]{1,0:T(8,128)(2,1)S(1)} collective-permute-done((bf16[128,1792]{1,0:T(8,128)(2,1)}, bf16[128,1792]{1,0:T(8,128)(2,1)S(1)}, u32[]{:S(2)}, u32[]{:S(2)}) %collective-permute-start.2) | collective-permute-done | bytes 458784 | tf_op jit(solution)/shard_map/ppermute | solution.py:22
  45.6 4.7 collective-permute-start.10
  50.4 5.1 %collective-permute-done.3 = bf16[128,1792]{1,0:T(8,128)(2,1)S(1)} collective-permute-done((bf16[128,1792]{1,0:T(8,128)(2,1)S(1)}, bf16[128,1792]{1,0:T(8,128)(2,1)S(1)}, u32[]{:S(2)}, u32[]{:S(2)}) %collective-permute-start.3) | collective-permute-done | bytes 458784 | tf_op jit(solution)/shard_map/ppermute | solution.py:22
  55.8 5.2 %collective-permute-start.11 = (bf16[128,1792]{1,0:T(8,128)(2,1)S(1)}, bf16[128,1792]{1,0:T(8,128)(2,1)S(1)}, u32[]{:S(2)}, u32[]{:S(2)}) collective-permute-start(bf16[128,1792]{1,0:T(8,128)(2,1)S(1)} %collective-permute-done.10), channel_id=1, source_target_pairs={{16,0},{32,16},{48,32},{64,48},{80,64},{96,80},{112,96},{128,112},... | collective-permute-start | bytes 1376264 | tf_op jit(solution)/shard_map/ppermute | solution.py:24
  61.0 5.1 %collective-permute-done.4 = bf16[128,1792]{1,0:T(8,128)(2,1)S(1)} collective-permute-done((bf16[128,1792]{1,0:T(8,128)(2,1)S(1)}, bf16[128,1792]{1,0:T(8,128)(2,1)S(1)}, u32[]{:S(2)}, u32[]{:S(2)}) %collective-permute-start.4) | collective-permute-done | bytes 458784 | tf_op jit(solution)/shard_map/ppermute | solution.py:22
  67.5 5.2 %collective-permute-start.12 = (bf16[128,1792]{1,0:T(8,128)(2,1)S(1)}, bf16[128,1792]{1,0:T(8,128)(2,1)}, u32[]{:S(2)}, u32[]{:S(2)}) collective-permute-start(bf16[128,1792]{1,0:T(8,128)(2,1)S(1)} %collective-permute-done.11), channel_id=1, source_target_pairs={{16,0},{32,16},{48,32},{64,48},{80,64},{96,80},{112,96},{128,112},... | collective-permute-start | bytes 1376264 | tf_op jit(solution)/shard_map/ppermute | solution.py:24
  72.8 4.9 collective-permute-done.5
  78.8 5.3 %collective-permute-start.13 = (bf16[128,1792]{1,0:T(8,128)(2,1)}, bf16[128,1792]{1,0:T(8,128)(2,1)}, u32[]{:S(2)}, u32[]{:S(2)}) collective-permute-start(bf16[128,1792]{1,0:T(8,128)(2,1)} %collective-permute-done.12), channel_id=1, source_target_pairs={{16,0},{32,16},{48,32},{64,48},{80,64},{96,80},{112,96},{128,112},... | collective-permute-start | bytes 1376264 | tf_op jit(solution)/shard_map/ppermute | solution.py:24
  84.2 6.2 %collective-permute-done.6 = bf16[128,1792]{1,0:T(8,128)(2,1)} collective-permute-done((bf16[128,1792]{1,0:T(8,128)(2,1)S(1)}, bf16[128,1792]{1,0:T(8,128)(2,1)}, u32[]{:S(2)}, u32[]{:S(2)}) %collective-permute-start.6) | collective-permute-done | bytes 458784 | tf_op jit(solution)/shard_map/ppermute | solution.py:22
  92.1 5.2 %collective-permute-start.14 = (bf16[128,1792]{1,0:T(8,128)(2,1)}, bf16[128,1792]{1,0:T(8,128)(2,1)}, u32[]{:S(2)}, u32[]{:S(2)}) collective-permute-start(bf16[128,1792]{1,0:T(8,128)(2,1)} %collective-permute-done.13), channel_id=1, source_target_pairs={{16,0},{32,16},{48,32},{64,48},{80,64},{96,80},{112,96},{128,112},... | collective-permute-start | bytes 1376264 | tf_op jit(solution)/shard_map/ppermute | solution.py:24
  97.3 6.8 %collective-permute-done.7 = bf16[128,1792]{1,0:T(8,128)(2,1)} collective-permute-done((bf16[128,1792]{1,0:T(8,128)(2,1)}, bf16[128,1792]{1,0:T(8,128)(2,1)}, u32[]{:S(2)}, u32[]{:S(2)}) %collective-permute-start.7) | collective-permute-done | bytes 458784 | tf_op jit(solution)/shard_map/ppermute | solution.py:22
  107.8 4.9 fusion.9
  112.8 1.9 bitcast_dynamic-update-slice_fusion.13
  114.7 1.9 bitcast_dynamic-update-slice_fusion.12
  118.4 1.8 bitcast_dynamic-update-slice_fusion.10
  122.1 1.8 bitcast_dynamic-update-slice_fusion.8
  125.7 1.8 bitcast_dynamic-update-slice_fusion.6
  131.8 1.8 bitcast_dynamic-update-slice_fusion.1
  135.4 7.1 %gather_fusion = bf16[16,128,1792]{2,1,0:T(8,128)(2,1)} fusion(bf16[16,128,1792]{2,1,0:T(8,128)(2,1)} %bitcast_dynamic-update-slice_fusion, s32[1024]{0:T(1024)S(1)} %pad_clamp_fusion), kind=kCustom, calls=%fused_computation | custom fusion | bytes 14680128 | tf_op jit(solution)/shard_map/gather | solution.py:27
  142.6 12.0 %convolution_bitcast_fusion = f32[896,2048]{0,1:T(8,128)} fusion(bf16[2048,1792]{1,0:T(8,128)(2,1)} %bitcast.49, bf16[1792,896]{1,0:T(8,128)(2,1)S(1)} %copy-done), kind=kOutput, calls=%fused_computation.10 | convolution fusion | flops 6576668672 | bytes 17891328 | tf_op jit(solution)/shard_map/dot_general | solution.py:31
  154.5 8.7 %copy.15 = f32[896,2048]{1,0:T(8,128)} copy(f32[896,2048]{0,1:T(8,128)} %convolution_bitcast_fusion) | data formatting | bytes 14680064
  163.3 38.6 %reduce-scatter.5.cloned.1.call-done = f32[128,512]{1,0:T(8,128)} async-done(((f32[2048,512]{1,0:T(8,128)}), f32[128,512]{1,0:T(8,128)}) %reduce-scatter.5.cloned.1.call-update) | async-done | bytes 262160 | tf_op jit(solution)/shard_map/reduce_scatter | solution.py:41
  203.6 67.8 %reduce-scatter.7.cloned.1.call-done = f32[56,2048]{1,0:T(8,128)} async-done(((f32[896,2048]{1,0:T(8,128)}), f32[56,2048]{1,0:T(8,128)}) %reduce-scatter.7.cloned.1.call-update) | async-done | bytes 458768 | tf_op jit(solution)/shard_map/reduce_scatter | solution.py:30
  273.4 51.2 %all-gather.8.cloned.1.call-done = bf16[2048,512]{1,0:T(8,128)(2,1)} async-done(((bf16[128,512]{1,0:T(8,128)(2,1)}), bf16[2048,512]{1,0:T(8,128)(2,1)}) %all-gather.8.cloned.1.call-update) | async-done | bytes 2097168 | tf_op jit(solution)/shard_map/all_gather | solution.py:47
  324.6 44.1 %all-gather.4.cloned.1.call-done = bf16[896,2048]{1,0:T(8,128)(2,1)} async-done(((bf16[56,2048]{1,0:T(8,128)(2,1)}), bf16[896,2048]{1,0:T(8,128)(2,1)}) %all-gather.4.cloned.1.call-update) | async-done | bytes 3670032 | tf_op jit(solution)/shard_map/all_gather | solution.py:38
  368.7 117.1 %while.14 = (s32[]{:T(128)}, f32[896,512]{1,0:T(8,128)}, s32[16]{0:T(128)S(1)}, bf16[896,2048]{1,0:T(8,128)(2,1)}, s32[16]{0:T(128)S(1)}, /*index=5*/bf16[2048,5...) while((s32[]{:T(128)}, f32[896,512]{1,0:T(8,128)}, s32[16]{0:T(128)S(1)}, ...), condition=%wide.region_4.5_spmd.clone, body=%wide.region_3.4_spmd.clone.sunk | while | flops 236389376 | bytes 4393164 | solution.py:68
  372.5 2.9 select_add_fusion.2
  379.3 3.5 select_add_fusion.2
  386.6 3.5 select_add_fusion.2
  394.0 3.5 select_add_fusion.2
  401.4 3.5 select_add_fusion.2
  408.8 3.5 select_add_fusion.2
  416.1 3.5 select_add_fusion.2
  423.5 3.5 select_add_fusion.2
  430.9 3.5 select_add_fusion.2
  438.2 3.5 select_add_fusion.2
  445.6 3.5 select_add_fusion.2
  453.0 3.5 select_add_fusion.2
  460.4 3.5 select_add_fusion.2
  467.7 3.5 select_add_fusion.2
  475.0 3.5 select_add_fusion.2
  482.3 3.5 select_add_fusion.2
  485.8 3.7 multiply_add_fusion
  (118 shorter events, 55.6 us)
Async XLA Ops:
  6.5 136.1 %copy-start = (bf16[1792,896]{1,0:T(8,128)(2,1)S(1)}, bf16[1792,896]{1,0:T(8,128)(2,1)}, u32[]{:S(2)}) copy-start(bf16[1792,896]{1,0:T(8,128)(2,1)} %param.10) | copy-start | bytes 9633796
  6.5 101.2 %all-gather.6.cloned.1.call-start = ((), (), s32[]{:S(2)}) async-start(), calls=%async_computation.3 | async-start | bytes 2228224 | tf_op jit(solution)/shard_map/all_gather | solution.py:40
  6.5 14.4 %collective-permute-start = (bf16[128,1792]{1,0:T(8,128)(2,1)}, bf16[128,1792]{1,0:T(8,128)(2,1)}, u32[]{:S(2)}, u32[]{:S(2)}) collective-permute-start(bf16[128,1792]{1,0:T(8,128)(2,1)} %param.8), channel_id=1, source_target_pairs={{0,16},{16,32},{32,48},{48,64},{64,80},{80,96},{96,112},{112,128},... | collective-permute-start | bytes 1376264 | tf_op jit(solution)/shard_map/ppermute | solution.py:22
  20.9 12.5 %collective-permute-start.1 = (bf16[128,1792]{1,0:T(8,128)(2,1)}, bf16[128,1792]{1,0:T(8,128)(2,1)}, u32[]{:S(2)}, u32[]{:S(2)}) collective-permute-start(bf16[128,1792]{1,0:T(8,128)(2,1)} %collective-permute-done), channel_id=1, source_target_pairs={{0,16},{16,32},{32,48},{48,64},{64,80},{80,96},{96,112},{112,128},... | collective-permute-start | bytes 1376264 | tf_op jit(solution)/shard_map/ppermute | solution.py:22
  20.9 181.0 %reduce-scatter.5.cloned.1.call-start = ((), (), s32[]{:S(2)}) async-start(), calls=%async_computation.4 | async-start | bytes 4456448 | tf_op jit(solution)/shard_map/reduce_scatter | solution.py:41
  21.0 12.4 %collective-permute-start.8 = (bf16[128,1792]{1,0:T(8,128)(2,1)}, bf16[128,1792]{1,0:T(8,128)(2,1)S(1)}, u32[]{:S(2)}, u32[]{:S(2)}) collective-permute-start(bf16[128,1792]{1,0:T(8,128)(2,1)} %param.8), channel_id=1, source_target_pairs={{16,0},{32,16},{48,32},{64,48},{80,64},{96,80},{112,96},{128,112},... | collective-permute-start | bytes 1376264 | tf_op jit(solution)/shard_map/ppermute | solution.py:24
  33.4 11.4 %collective-permute-start.2 = (bf16[128,1792]{1,0:T(8,128)(2,1)}, bf16[128,1792]{1,0:T(8,128)(2,1)S(1)}, u32[]{:S(2)}, u32[]{:S(2)}) collective-permute-start(bf16[128,1792]{1,0:T(8,128)(2,1)} %collective-permute-done.1), channel_id=1, source_target_pairs={{0,16},{16,32},{32,48},{48,64},{64,80},{80,96},{96,112},{112,128},... | collective-permute-start | bytes 1376264 | tf_op jit(solution)/shard_map/ppermute | solution.py:22
  33.4 0.8 copy-start.1
  34.2 10.7 %collective-permute-start.9 = (bf16[128,1792]{1,0:T(8,128)(2,1)S(1)}, bf16[128,1792]{1,0:T(8,128)(2,1)S(1)}, u32[]{:S(2)}, u32[]{:S(2)}) collective-permute-start(bf16[128,1792]{1,0:T(8,128)(2,1)S(1)} %collective-permute-done.8), channel_id=1, source_target_pairs={{16,0},{32,16},{48,32},{64,48},{80,64},{96,80},{112,96},{128,112},... | collective-permute-start | bytes 1376264 | tf_op jit(solution)/shard_map/ppermute | solution.py:24
  44.8 11.0 %copy-start.4 = (bf16[128,1792]{1,0:T(8,128)(2,1)}, bf16[128,1792]{1,0:T(8,128)(2,1)S(1)}, u32[]{:S(2)}) copy-start(bf16[128,1792]{1,0:T(8,128)(2,1)S(1)} %collective-permute-done.2) | copy-start | bytes 1376260
  44.8 10.6 %collective-permute-start.3 = (bf16[128,1792]{1,0:T(8,128)(2,1)S(1)}, bf16[128,1792]{1,0:T(8,128)(2,1)S(1)}, u32[]{:S(2)}, u32[]{:S(2)}) collective-permute-start(bf16[128,1792]{1,0:T(8,128)(2,1)S(1)} %collective-permute-done.2), channel_id=1, source_target_pairs={{0,16},{16,32},{32,48},{48,64},{64,80},{80,96},{96,112},{112,128},... | collective-permute-start | bytes 1376264 | tf_op jit(solution)/shard_map/ppermute | solution.py:22
  44.8 0.8 copy-start.2
  45.6 10.2 %collective-permute-start.10 = (bf16[128,1792]{1,0:T(8,128)(2,1)S(1)}, bf16[128,1792]{1,0:T(8,128)(2,1)S(1)}, u32[]{:S(2)}, u32[]{:S(2)}) collective-permute-start(bf16[128,1792]{1,0:T(8,128)(2,1)S(1)} %collective-permute-done.9), channel_id=1, source_target_pairs={{16,0},{32,16},{48,32},{64,48},{80,64},{96,80},{112,96},{128,112},... | collective-permute-start | bytes 1376264 | tf_op jit(solution)/shard_map/ppermute | solution.py:24
  55.4 23.4 %copy-start.9 = (bf16[128,1792]{1,0:T(8,128)(2,1)}, bf16[128,1792]{1,0:T(8,128)(2,1)S(1)}, u32[]{:S(2)}) copy-start(bf16[128,1792]{1,0:T(8,128)(2,1)S(1)} %collective-permute-done.3) | copy-start | bytes 1376260
  55.5 10.6 %collective-permute-start.4 = (bf16[128,1792]{1,0:T(8,128)(2,1)S(1)}, bf16[128,1792]{1,0:T(8,128)(2,1)S(1)}, u32[]{:S(2)}, u32[]{:S(2)}) collective-permute-start(bf16[128,1792]{1,0:T(8,128)(2,1)S(1)} %collective-permute-done.3), channel_id=1, source_target_pairs={{0,16},{16,32},{32,48},{48,64},{64,80},{80,96},{96,112},{112,128},... | collective-permute-start | bytes 1376264 | tf_op jit(solution)/shard_map/ppermute | solution.py:22
  55.8 5.2 %copy-start.5 = (bf16[128,1792]{1,0:T(8,128)(2,1)}, bf16[128,1792]{1,0:T(8,128)(2,1)S(1)}, u32[]{:S(2)}) copy-start(bf16[128,1792]{1,0:T(8,128)(2,1)S(1)} %collective-permute-done.10) | copy-start | bytes 1376260
  55.8 11.0 %collective-permute-start.11 = (bf16[128,1792]{1,0:T(8,128)(2,1)S(1)}, bf16[128,1792]{1,0:T(8,128)(2,1)S(1)}, u32[]{:S(2)}, u32[]{:S(2)}) collective-permute-start(bf16[128,1792]{1,0:T(8,128)(2,1)S(1)} %collective-permute-done.10), channel_id=1, source_target_pairs={{16,0},{32,16},{48,32},{64,48},{80,64},{96,80},{112,96},{128,112},... | collective-permute-start | bytes 1376264 | tf_op jit(solution)/shard_map/ppermute | solution.py:24
  66.1 18.1 %copy-start.10 = (bf16[128,1792]{1,0:T(8,128)(2,1)}, bf16[128,1792]{1,0:T(8,128)(2,1)S(1)}, u32[]{:S(2)}) copy-start(bf16[128,1792]{1,0:T(8,128)(2,1)S(1)} %collective-permute-done.4) | copy-start | bytes 1376260
  66.1 11.6 %collective-permute-start.5 = (bf16[128,1792]{1,0:T(8,128)(2,1)S(1)}, bf16[128,1792]{1,0:T(8,128)(2,1)S(1)}, u32[]{:S(2)}, u32[]{:S(2)}) collective-permute-start(bf16[128,1792]{1,0:T(8,128)(2,1)S(1)} %collective-permute-done.4), channel_id=1, source_target_pairs={{0,16},{16,32},{32,48},{48,64},{64,80},{80,96},{96,112},{112,128},... | collective-permute-start | bytes 1376264 | tf_op jit(solution)/shard_map/ppermute | solution.py:22
  66.8 0.8 copy-start.7
  67.5 11.3 %collective-permute-start.12 = (bf16[128,1792]{1,0:T(8,128)(2,1)S(1)}, bf16[128,1792]{1,0:T(8,128)(2,1)}, u32[]{:S(2)}, u32[]{:S(2)}) collective-permute-start(bf16[128,1792]{1,0:T(8,128)(2,1)S(1)} %collective-permute-done.11), channel_id=1, source_target_pairs={{16,0},{32,16},{48,32},{64,48},{80,64},{96,80},{112,96},{128,112},... | collective-permute-start | bytes 1376264 | tf_op jit(solution)/shard_map/ppermute | solution.py:24
  77.7 12.7 %copy-start.11 = (bf16[128,1792]{1,0:T(8,128)(2,1)}, bf16[128,1792]{1,0:T(8,128)(2,1)S(1)}, u32[]{:S(2)}) copy-start(bf16[128,1792]{1,0:T(8,128)(2,1)S(1)} %collective-permute-done.5) | copy-start | bytes 1376260
  77.7 12.7 %collective-permute-start.6 = (bf16[128,1792]{1,0:T(8,128)(2,1)S(1)}, bf16[128,1792]{1,0:T(8,128)(2,1)}, u32[]{:S(2)}, u32[]{:S(2)}) collective-permute-start(bf16[128,1792]{1,0:T(8,128)(2,1)S(1)} %collective-permute-done.5), channel_id=1, source_target_pairs={{0,16},{16,32},{32,48},{48,64},{64,80},{80,96},{96,112},{112,128},... | collective-permute-start | bytes 1376264 | tf_op jit(solution)/shard_map/ppermute | solution.py:22
  78.8 13.2 %collective-permute-start.13 = (bf16[128,1792]{1,0:T(8,128)(2,1)}, bf16[128,1792]{1,0:T(8,128)(2,1)}, u32[]{:S(2)}, u32[]{:S(2)}) collective-permute-start(bf16[128,1792]{1,0:T(8,128)(2,1)} %collective-permute-done.12), channel_id=1, source_target_pairs={{16,0},{32,16},{48,32},{64,48},{80,64},{96,80},{112,96},{128,112},... | collective-permute-start | bytes 1376264 | tf_op jit(solution)/shard_map/ppermute | solution.py:24
  90.4 13.7 %collective-permute-start.7 = (bf16[128,1792]{1,0:T(8,128)(2,1)}, bf16[128,1792]{1,0:T(8,128)(2,1)}, u32[]{:S(2)}, u32[]{:S(2)}) collective-permute-start(bf16[128,1792]{1,0:T(8,128)(2,1)} %collective-permute-done.6), channel_id=1, source_target_pairs={{0,16},{16,32},{32,48},{48,64},{64,80},{80,96},{96,112},{112,128},... | collective-permute-start | bytes 1376264 | tf_op jit(solution)/shard_map/ppermute | solution.py:22
  92.1 41.6 %collective-permute-start.14 = (bf16[128,1792]{1,0:T(8,128)(2,1)}, bf16[128,1792]{1,0:T(8,128)(2,1)}, u32[]{:S(2)}, u32[]{:S(2)}) collective-permute-start(bf16[128,1792]{1,0:T(8,128)(2,1)} %collective-permute-done.13), channel_id=1, source_target_pairs={{16,0},{32,16},{48,32},{64,48},{80,64},{96,80},{112,96},{128,112},... | collective-permute-start | bytes 1376264 | tf_op jit(solution)/shard_map/ppermute | solution.py:24
  112.7 158.7 %reduce-scatter.7.cloned.1.call-start = ((), (), s32[]{:S(2)}) async-start(), calls=%async_computation.6 | async-start | bytes 7798784 | tf_op jit(solution)/shard_map/reduce_scatter | solution.py:30
  112.8 14.8 %copy-start.3 = (bf16[128,1792]{1,0:T(8,128)(2,1)S(1)}, bf16[128,1792]{1,0:T(8,128)(2,1)}, u32[]{:S(2)}) copy-start(bf16[128,1792]{1,0:T(8,128)(2,1)} %copy-done.2) | copy-start | bytes 1376260
  112.8 15.6 %copy-start.6 = (bf16[128,1792]{1,0:T(8,128)(2,1)S(1)}, bf16[128,1792]{1,0:T(8,128)(2,1)}, u32[]{:S(2)}) copy-start(bf16[128,1792]{1,0:T(8,128)(2,1)} %copy-done.5) | copy-start | bytes 1376260
  112.8 16.4 %copy-start.8 = (bf16[128,1792]{1,0:T(8,128)(2,1)S(1)}, bf16[128,1792]{1,0:T(8,128)(2,1)}, u32[]{:S(2)}) copy-start(bf16[128,1792]{1,0:T(8,128)(2,1)} %copy-done.7) | copy-start | bytes 1376260
  163.2 109.9 %copy-start.12 = (s32[16]{0:T(128)S(1)}, s32[16]{0:T(128)}, u32[]{:S(2)}) copy-start(s32[16]{0:T(128)} %param.13) | copy-start | bytes 196
  163.3 161.3 %all-gather.8.cloned.1.call-start = ((), (), s32[]{:S(2)}) async-start(), calls=%async_computation.5 | async-start | bytes 2228224 | tf_op jit(solution)/shard_map/all_gather | solution.py:47
  203.5 165.2 %all-gather.4.cloned.1.call-start = ((), (), s32[]{:S(2)}) async-start(), calls=%async_computation.2 | async-start | bytes 3899392 | tf_op jit(solution)/shard_map/all_gather | solution.py:38
Sparse Core Ops, SparseCore 0:
  21.0 45.1 all-gather.5
  112.8 89.0 reduce-scatter.4
  204.6 66.7 reduce-scatter.6
  274.0 50.5 all-gather.7
  326.4 42.2 all-gather.3
